TPU v7x, 512 devices: a whole 4x4x16 slice. The times are simulated.
512 devices in a mesh: gx: 8 (over z_lo), gy: 8 (over y, z_hi), gz: 8 (over x, core).
Axes of the slice: x: 4, y: 4, z: 16 (z_hi: 2, z_lo: 8; z = z_hi * 8 + z_lo), core: 2. Of those that a mesh axis runs over, the one named last changes fastest.
Arguments:
- mid_stream: bfloat16 [1024, 7168], P('gz', ('gx', 'gy')), may hold values from -6 to 6
- out_grad: bfloat16 [1024, 7168], P('gz', ('gx', 'gy')), may hold values from -6 to 6
- attn_values: bfloat16 [1024, 7168], P(('gz', 'gx'), 'gy'), may hold values from -6 to 6
- attn_gate: bfloat16 [7168], P(('gx', 'gy')), may hold values from 0.099609375 to 1.8984375
- ffn_gate: bfloat16 [7168], P(('gx', 'gy')), may hold values from 0.099609375 to 1.8984375
- up_weight: bfloat16 [14336, 7168], P(('gy', 'gz'), 'gx'), may hold values from -0.0625 to 0.0625
- down_weight: bfloat16 [14336, 7168], P(('gy', 'gz'), 'gx'), may hold values from -0.046875 to 0.046875
- proj_weight: bfloat16 [7168, 7168], P(('gx', 'gz'), 'gy'), may hold values from -0.0625 to 0.0625
Outputs:
- grad_mid: bfloat16 [1024, 7168], P('gz', ('gx', 'gy'))
- grad_attn: bfloat16 [1024, 7168], P(('gz', 'gx'), 'gy')
- grad_proj: bfloat16 [7168, 7168], P(('gx', 'gz'), 'gy')
- grad_up: bfloat16 [14336, 7168], P(('gy', 'gz'), 'gx')
- grad_down: bfloat16 [14336, 7168], P(('gy', 'gz'), 'gx')
All inputs are finite; a program needn't handle non-finite values.
Results may differ from a plain program's by a relative error of at most 0.025.
Values may be sent and summed in bfloat16 or wider, within the bound.
A program may use at most 64 MiB of HBM per device.

v0:
```python
import jax
import jax.numpy as jnp
from jax import lax
from jax.sharding import PartitionSpec as P

root_two_pi = 0.7978845608028654
cubic_term = 0.044715


def gelu_value(values):
    inside = root_two_pi * (values + cubic_term * values * values * values)
    return 0.5 * values * (1.0 + jnp.tanh(inside))


def gelu_slope(values):
    tangent = jnp.tanh(root_two_pi * (values + cubic_term * values * values * values))
    return 0.5 * (1.0 + tangent) + 0.5 * values * (1.0 - tangent * tangent) * root_two_pi * (
        1.0 + 3.0 * cubic_term * values * values
    )


def matmul(former, latter):
    return jnp.dot(former, latter, preferred_element_type=jnp.float32)


def trans_times(former, latter):
    return lax.dot_general(
        former, latter, (((1,), (1,)), ((), ())), preferred_element_type=jnp.float32
    )


def trans_left(former, latter):
    return lax.dot_general(
        former, latter, (((0,), (0,)), ((), ())), preferred_element_type=jnp.float32
    )


def per_device(
    mid_stream, out_grad, attn_values, attn_gate, ffn_gate, up_weight, down_weight, proj_weight
):
    tok_total = mid_stream.shape[0] * lax.axis_size("gz")
    factor = float(tok_total) ** (-0.5)
    gated_grad = (out_grad.astype(jnp.float32) * ffn_gate.astype(jnp.float32)).astype(jnp.bfloat16)
    mid_columns, gated_columns = (
        lax.all_gather(mid_stream, "gy", axis=1, tiled=True),
        lax.all_gather(gated_grad, "gy", axis=1, tiled=True),
    )
    up_block, down_block, proj_block = (
        lax.all_gather(up_weight, "gz", axis=0, tiled=True),
        lax.all_gather(down_weight, "gz", axis=0, tiled=True),
        lax.all_gather(proj_weight, "gz", axis=0, tiled=True),
    )
    down_part = trans_times(gated_columns, down_block)
    up_part = trans_times(mid_columns, up_block)
    pre_gelu, gelu_grad = (
        lax.psum_scatter(
            up_part.astype(jnp.bfloat16), "gx", scatter_dimension=1, tiled=True
        ).astype(jnp.float32),
        lax.psum_scatter(
            down_part.astype(jnp.bfloat16), "gx", scatter_dimension=1, tiled=True
        ).astype(jnp.float32),
    )
    hidden = gelu_value(pre_gelu).astype(jnp.bfloat16)
    hidden_grad = (gelu_grad * gelu_slope(pre_gelu)).astype(jnp.bfloat16)
    hidden_columns, grad_columns, attn_rows = (
        lax.all_gather(hidden, "gx", axis=1, tiled=True),
        lax.all_gather(hidden_grad, "gx", axis=1, tiled=True),
        lax.all_gather(attn_values, "gx", axis=0, tiled=True),
    )
    hidden_tokens, grad_tokens = (
        lax.all_to_all(hidden_columns, "gz", split_axis=1, concat_axis=0, tiled=True),
        lax.all_to_all(grad_columns, "gz", split_axis=1, concat_axis=0, tiled=True),
    )
    mid_tokens, gated_tokens, attn_tokens = (
        lax.all_gather(mid_columns, "gz", axis=0, tiled=True),
        lax.all_gather(gated_columns, "gz", axis=0, tiled=True),
        lax.all_gather(attn_rows, "gz", axis=0, tiled=True),
    )
    grad_up = (trans_left(grad_tokens, mid_tokens) * factor).astype(jnp.bfloat16)
    grad_down = (trans_left(hidden_tokens, gated_tokens) * factor).astype(jnp.bfloat16)
    back_part = matmul(grad_columns, up_block)
    back_sum = lax.psum_scatter(
        back_part.astype(jnp.bfloat16), "gy", scatter_dimension=1, tiled=True
    ).astype(jnp.float32)
    mid_total = out_grad.astype(jnp.float32) + back_sum
    grad_mid = mid_total.astype(jnp.bfloat16)
    gated_mid = (mid_total * attn_gate.astype(jnp.float32)).astype(jnp.bfloat16)
    gated_mid_columns = lax.all_gather(gated_mid, "gy", axis=1, tiled=True)
    gated_mid_tokens = lax.all_to_all(
        gated_mid_columns, "gz", split_axis=1, concat_axis=0, tiled=True
    )
    grad_proj = (trans_left(gated_mid_tokens, attn_tokens) * factor).astype(jnp.bfloat16)
    attn_part = matmul(gated_mid_columns, proj_block)
    grad_attn = lax.psum_scatter(
        attn_part.astype(jnp.bfloat16), "gx", scatter_dimension=0, tiled=True
    )
    return (grad_mid, grad_attn, grad_proj, grad_up, grad_down)


def solution(mesh):
    return jax.shard_map(
        per_device,
        mesh=mesh,
        in_specs=(
            P("gz", ("gx", "gy")),
            P("gz", ("gx", "gy")),
            P(("gz", "gx"), "gy"),
            P(("gx", "gy")),
            P(("gx", "gy")),
            P(("gy", "gz"), "gx"),
            P(("gy", "gz"), "gx"),
            P(("gx", "gz"), "gy"),
        ),
        out_specs=(
            P("gz", ("gx", "gy")),
            P(("gz", "gx"), "gy"),
            P(("gx", "gz"), "gy"),
            P(("gy", "gz"), "gx"),
            P(("gy", "gz"), "gx"),
        ),
        check_vma=False,
    )
```

profile of v0, /device:TPU:4, one launch (start us, length us, event | category | flops | bytes accessed | tf_op | source)
XLA Modules:
  0.0 538.8 jit_solution(12020783953984760049)
XLA Ops:
  7.9 0.7 all-gather.7.cloned.1.call-update
  8.7 67.4 %all_gather.38 = bf16[128,896]{0,1:T(8,128)(2,1)S(1)} all-gather(bf16[128,112]{0,1:T(8,128)(2,1)} %param.8), channel_id=1, replica_groups=mesh['gx'=8,'gy'=8,'gz'=8] {'gy'}, dimensions={1}, use_global_device_ids=true | all-gather | bytes 258048 | tf_op jit(solution)/shard_map/all_gather | solution.py:45
  76.1 3.8 convolution_convert_fusion
  80.1 64.1 %all_gather.36 = bf16[128,896]{0,1:T(8,128)(2,1)S(1)} all-gather(bf16[128,112]{0,1:T(8,128)(2,1)S(1)} %fusion.20), channel_id=1, replica_groups=mesh['gx'=8,'gy'=8,'gz'=8] {'gy'}, dimensions={1}, use_global_device_ids=true | all-gather | bytes 258048 | tf_op jit(solution)/shard_map/all_gather | solution.py:46
  144.2 3.8 convolution_convert_fusion.1
  148.8 8.5 %reduce-scatter.7.cloned.1.call-done = bf16[128,224]{0,1:T(8,128)(2,1)} async-done(((bf16[128,1792]{0,1:T(8,128)(2,1)}), bf16[128,224]{0,1:T(8,128)(2,1)}) %reduce-scatter.7.cloned.1.call-update) | async-done | bytes 57360 | tf_op jit(solution)/shard_map/reduce_scatter | solution.py:56
  157.2 60.0 %reduce-scatter.5.cloned.1.call-done = bf16[128,224]{0,1:T(8,128)(2,1)} async-done(((bf16[128,1792]{0,1:T(8,128)(2,1)}), bf16[128,224]{0,1:T(8,128)(2,1)}) %reduce-scatter.5.cloned.1.call-update) | async-done | bytes 57360 | tf_op jit(solution)/shard_map/reduce_scatter | solution.py:59
  217.2 0.9 fusion.16
  218.2 47.8 %all_gather.40 = bf16[128,1792]{0,1:T(8,128)(2,1)S(1)} all-gather(bf16[128,224]{0,1:T(8,128)(2,1)S(1)} %get-tuple-element.6), channel_id=1, replica_groups=mesh['gx'=8,'gy'=8,'gz'=8] {'gx'}, dimensions={1}, use_global_device_ids=true | all-gather | bytes 516096 | tf_op jit(solution)/shard_map/all_gather | solution.py:67
  265.9 0.8 copy-done.1
  266.7 2.1 convolution_convert_fusion.3
  270.4 48.8 %all_gather.43 = bf16[128,896]{1,0:T(8,128)(2,1)} all-gather(bf16[16,896]{1,0:T(8,128)(2,1)S(1)} %copy-done.5), channel_id=1, replica_groups=mesh['gx'=8,'gy'=8,'gz'=8] {'gx'}, dimensions={0}, use_global_device_ids=true | all-gather | bytes 258048 | tf_op jit(solution)/shard_map/all_gather | solution.py:68
  319.2 4.8 all-to-all-start.1
  324.0 49.7 %all_gather.46 = bf16[128,1792]{0,1:T(8,128)(2,1)} all-gather(bf16[128,224]{0,1:T(8,128)(2,1)S(1)} %get-tuple-element.5), channel_id=1, replica_groups=mesh['gx'=8,'gy'=8,'gz'=8] {'gx'}, dimensions={1}, use_global_device_ids=true | all-gather | bytes 516096 | tf_op jit(solution)/shard_map/all_gather | solution.py:66
  373.7 4.8 all-to-all-start.2
  378.5 3.1 fusion
  381.6 1.4 multiply_convert_fusion
  382.9 66.6 %all_gather.41 = bf16[128,896]{0,1:T(8,128)(2,1)} all-gather(bf16[128,112]{0,1:T(8,128)(2,1)S(1)} %get-tuple-element.7), channel_id=1, replica_groups=mesh['gx'=8,'gy'=8,'gz'=8] {'gy'}, dimensions={1}, use_global_device_ids=true | all-gather | bytes 258048 | tf_op jit(solution)/shard_map/all_gather | solution.py:88
  449.6 2.7 convolution_convert_fusion.2
  452.4 4.8 all-to-all-start
  457.2 3.0 fusion.1
  460.2 2.4 all-gather.13.cloned.1.call-done
  462.6 2.6 fusion.2
  465.2 66.7 %reduce-scatter.11.cloned.1.call-done = bf16[16,896]{1,0:T(8,128)(2,1)} async-done(((bf16[128,896]{1,0:T(8,128)(2,1)}), bf16[16,896]{1,0:T(8,128)(2,1)}) %reduce-scatter.11.cloned.1.call-update) | async-done | bytes 28688 | tf_op jit(solution)/shard_map/reduce_scatter | solution.py:94
  (46 shorter events, 3.2 us)
Async XLA Ops:
  7.2 68.9 %all-gather.9.cloned.1.call-start = ((), (), s32[]{:S(2)}) async-start(), calls=%async_computation.9 | async-start | bytes 3612672 | tf_op jit(solution)/shard_map/all_gather | solution.py:49
  7.9 136.3 %all-gather.7.cloned.1.call-start = ((), (), s32[]{:S(2)}) async-start(), calls=%async_computation.7 | async-start | bytes 3612672 | tf_op jit(solution)/shard_map/all_gather | solution.py:50
  8.6 148.6 %reduce-scatter.7.cloned.1.call-start = ((), (), s32[]{:S(2)}) async-start(), calls=%async_computation.10 | async-start | bytes 516096 | tf_op jit(solution)/shard_map/reduce_scatter | solution.py:56
  76.0 3.9 copy-start.3
  76.0 3.9 copy-start.6
  76.1 4.0 copy-start.4
  79.9 137.3 %reduce-scatter.5.cloned.1.call-start = ((), (), s32[]{:S(2)}) async-start(), calls=%async_computation.8 | async-start | bytes 516096 | tf_op jit(solution)/shard_map/reduce_scatter | solution.py:59
  144.2 3.9 copy-start.2
  144.2 122.5 %copy-start = (bf16[1792,896]{1,0:T(8,128)(2,1)S(1)}, bf16[1792,896]{1,0:T(8,128)(2,1)}, u32[]{:S(2)}) copy-start(bf16[1792,896]{1,0:T(8,128)(2,1)} %all-gather.9.cloned.1.call-done) | copy-start | bytes 9633796
  148.1 230.4 %all-gather.15.cloned.1.call-start = ((), (), s32[]{:S(2)}) async-start(), calls=%async_computation.15 | async-start | bytes 2064384 | tf_op jit(solution)/shard_map/all_gather | solution.py:75
  148.7 232.9 %reduce-scatter.9.cloned.1.call-start = ((), (), s32[]{:S(2)}) async-start(), calls=%async_computation.11 | async-start | bytes 258048 | tf_op jit(solution)/shard_map/reduce_scatter | solution.py:82
  265.9 0.8 copy-start.1
  266.7 3.6 copy-start.5
  268.8 55.2 %copy-start.7 = (bf16[112]{0:T(256)(128)(2,1)S(1)}, bf16[112]{0:T(256)(128)(2,1)}, u32[]{:S(2)}) copy-start(bf16[112]{0:T(256)(128)(2,1)} %param.11) | copy-start | bytes 676
  268.8 180.7 %all-gather.11.cloned.1.call-start = ((), (), s32[]{:S(2)}) async-start(), calls=%async_computation.12 | async-start | bytes 1806336 | tf_op jit(solution)/shard_map/all_gather | solution.py:51
  269.6 187.6 %all-gather.17.cloned.1.call-start = ((), (), s32[]{:S(2)}) async-start(), calls=%async_computation.16 | async-start | bytes 2064384 | tf_op jit(solution)/shard_map/all_gather | solution.py:76
  270.3 192.3 %all-gather.13.cloned.1.call-start = ((), (), s32[]{:S(2)}) async-start(), calls=%async_computation.14 | async-start | bytes 2064384 | tf_op jit(solution)/shard_map/all_gather | solution.py:77
  319.2 54.5 %all-to-all-start.1 = ((bf16[128,8,224]{0,2,1:T(8,128)(2,1)}), bf16[128,8,224]{0,2,1:T(8,128)(2,1)S(1)}, u32[]{:S(2)}, u32[]{:S(2)}) async-start(bf16[128,8,224]{0,2,1:T(8,128)(2,1)} %bitcast.38), calls=%async_computation.5 | async-start | bytes 917504 | tf_op jit(solution)/shard_map/all_to_all | solution.py:72
  373.7 78.6 %all-to-all-start.2 = ((bf16[128,8,224]{0,2,1:T(8,128)(2,1)}), bf16[128,8,224]{0,2,1:T(8,128)(2,1)S(1)}, u32[]{:S(2)}, u32[]{:S(2)}) async-start(bf16[128,8,224]{0,2,1:T(8,128)(2,1)} %bitcast.4), calls=%async_computation.6 | async-start | bytes 917504 | tf_op jit(solution)/shard_map/all_to_all | solution.py:71
  378.5 153.4 %reduce-scatter.11.cloned.1.call-start = ((), (), s32[]{:S(2)}) async-start(), calls=%async_computation.13 | async-start | bytes 258048 | tf_op jit(solution)/shard_map/reduce_scatter | solution.py:94
  452.4 10.2 %all-to-all-start = ((bf16[128,8,112]{0,2,1:T(8,128)(2,1)}), bf16[128,8,112]{0,2,1:T(8,128)(2,1)S(1)}, u32[]{:S(2)}, u32[]{:S(2)}) async-start(bf16[128,8,112]{0,2,1:T(8,128)(2,1)} %bitcast), calls=%async_computation.4 | async-start | bytes 458752 | tf_op jit(solution)/shard_map/all_to_all | solution.py:89
Sparse Core Ops, SparseCore 0:
  10.1 38.7 all-gather.8
  51.0 35.6 all-gather.6
  89.5 67.6 reduce-scatter.6
  160.1 57.0 reduce-scatter.4
  219.8 27.1 all-gather.14
  268.9 95.4 reduce-scatter.8
  366.6 24.4 all-gather.10
  393.2 33.5 all-gather.16
  428.9 33.6 all-gather.12
  465.8 66.0 reduce-scatter.10
where the time goes:
time: 539 us
  blocking collectives  344 us (64%)
  waiting for transfers between devices  141 us (26%)
  matrix products  21.2 us (4%)
  starting transfers between devices  14.8 us (3%)
  between operations  14.2 us (3%)
    all_gather x1, blocking collectives, per_device(): lax.all_gather(mid_stream, 'gy', axis=1, tiled=True)  67.4 us
    reduce_scatter x1, waiting for transfers between devices, per_device(): lax.psum_scatter(attn_part.astype(jnp.bfloat16), 'gx', scatter_dimension=...  66.7 us
    all_gather x1, blocking collectives, per_device(): gated_mid_columns = lax.all_gather(gated_mid, 'gy', axis=1, tiled=True)  66.6 us
    all_gather x1, blocking collectives, per_device(): lax.all_gather(gated_grad, 'gy', axis=1, tiled=True)  64.1 us
    reduce_scatter x1, waiting for transfers between devices, per_device(): lax.psum_scatter(down_part.astype(jnp.bfloat16), 'gx', scatter_dimension=...  60 us
    all_gather x1, blocking collectives, per_device(): lax.all_gather(hidden, 'gx', axis=1, tiled=True)  49.7 us
    all_gather x1, blocking collectives, per_device(): lax.all_gather(attn_values, 'gx', axis=0, tiled=True)  48.8 us
    all_gather x1, blocking collectives, per_device(): lax.all_gather(hidden_grad, 'gx', axis=1, tiled=True)  47.8 us
  transfers between devices with their start and end apart: 13, of which 4 were waited for; matrix products, arithmetic and copies ran while one was open for 4% of the time, Pallas kernels for 0%

commit v1 on v0

v1 whole, which is shorter than its diff:
```python
import functools

import jax
import jax.numpy as jnp
from jax import lax
from jax.experimental import pallas as pl
from jax.experimental.pallas import tpu as pltpu
from jax.sharding import PartitionSpec as P

MESH = pl.DeviceIdType.MESH
BF16, F32 = jnp.bfloat16, jnp.float32
root_two_pi = 0.7978845608028654
cubic_term = 0.044715


def dot(former, latter, contract):
    return lax.dot_general(
        former, latter, ((contract[:1], contract[1:]), ((), ())), preferred_element_type=F32
    )


def gelu_pair(values):
    square = values * values
    tangent = jnp.tanh(root_two_pi * (values + cubic_term * values * square))
    half = 0.5 * (1.0 + tangent)
    slope = half + 0.5 * values * (1.0 - tangent * tangent) * root_two_pi * (
        1.0 + 3.0 * cubic_term * square
    )
    return values * half, slope


def kernel(
    factor,
    mid_ref, out_ref, attn_ref, agate_ref, fgate_ref, up_ref, down_ref, proj_ref,
    gmid_ref, gattn_ref, gproj_ref, gup_ref, gdown_ref,
    G, part, from_outer, from_mid, H, up_all, proj_all, attn_all, gates, og_t,
    HG, back, tot, back_send, yr, t_send, hr, GM, GP, ap, ar, acc,
    rs_s, rs_r, xm_s, xm_r, ag_s, ag_r, dp_s, dp_r, send_sems, recv_sems,
):
    feats, toks = mid_ref.shape[1], mid_ref.shape[0]
    units = up_ref.shape[0]
    a = lax.axis_index("gx")
    gy = lax.axis_index("gy")
    gz = lax.axis_index("gz")
    x, c = gz // 2, lax.rem(gz, 2)
    y, h = gy // 2, lax.rem(gy, 2)

    def xpeer(d):
        return {"gz": lax.rem(x + d, 4) * 2 + c}

    def ypeer(d):
        return {"gy": lax.rem(y + d, 4) * 2 + h}

    core = {"gz": x * 2 + 1 - c}
    hpeer = {"gy": y * 2 + 1 - h}

    def gxpeer(d):
        return {"gx": lax.rem(a + d, 8)}

    def gzpeer(d):
        return {"gz": lax.rem(gz + d, 8)}

    barrier = pltpu.get_barrier_semaphore()
    peers = [gzpeer(d) for d in range(1, 8)] + [gxpeer(d) for d in range(1, 8)]
    peers += [ypeer(d) for d in range(1, 4)] + [hpeer]
    for peer in peers:
        pl.semaphore_signal(barrier, inc=1, device_id=peer, device_id_type=MESH)

    sent = []
    count = [0]

    def put(src, dst, peer):
        index = count[0]
        count[0] += 1
        copy = pltpu.make_async_remote_copy(
            src, dst, send_sems.at[index], recv_sems.at[index],
            device_id=peer, device_id_type=MESH,
        )
        copy.start()
        sent.append(copy)
        return copy

    lanes = pl.ds(pl.multiple_of(c * toks, toks), toks)
    other_lanes = pl.ds(pl.multiple_of((1 - c) * toks, toks), toks)
    own_rows = pl.ds(pl.multiple_of(gy * feats, 16), feats)
    y_rows = pl.ds(pl.multiple_of(y * 2 * feats, 32), 2 * feats)
    h_rows = pl.ds(pl.multiple_of(h * feats, 16), feats)

    out_grad = out_ref[...].astype(F32)
    gated = (out_grad * fgate_ref[...].astype(F32)).astype(BF16).astype(F32)
    G[x, 0, own_rows, lanes] = mid_ref[...].astype(F32).T.astype(BF16)
    G[x, 1, own_rows, lanes] = gated.T.astype(BF16)
    og_t[...] = out_grad.T
    gates[h_rows, :] = jnp.broadcast_to(agate_ref[...].astype(F32), (toks, feats)).T.astype(BF16)

    pl.semaphore_wait(barrier, len(peers))

    h_copy = put(G.at[x, :, own_rows, lanes], G.at[x, :, own_rows, lanes], hpeer)
    gate_copy = put(gates.at[h_rows, :], gates.at[h_rows, :], hpeer)
    attn_row = pl.ds(pl.multiple_of((gz * 8 + a) * 16, 16), 16)
    attn_all[attn_row, :] = attn_ref[...]
    up_all[gz] = up_ref[...]
    proj_all[gz] = proj_ref[...]
    h_copy.wait_recv()
    mid_y = [put(G.at[x, 0, y_rows, lanes], G.at[x, 0, y_rows, lanes], ypeer(d)) for d in (1, 3, 2)]
    gat_x = [put(G.at[x, 1, y_rows, lanes], G.at[x, 1, y_rows, lanes], xpeer(d)) for d in (1, 3, 2)]
    attn_z = [put(attn_ref, attn_all.at[attn_row, :], gxpeer(d)) for d in range(1, 8)]
    for copy in mid_y:
        copy.wait_recv()
    mid_x = [put(G.at[x, 0, :, lanes], G.at[x, 0, :, lanes], xpeer(d)) for d in (1, 3, 2)]
    mid_c = [put(G.at[x, 0, :, lanes], G.at[x, 0, :, lanes], core)]
    for copy in gat_x:
        copy.wait_recv()
    gat_y = [put(G.at[:, 1, y_rows, lanes], G.at[:, 1, y_rows, lanes], ypeer(d)) for d in (1, 3, 2)]
    for copy, d in zip(mid_x, (1, 3, 2)):
        copy.wait_recv()
        block = lax.rem(x - d + 4, 4)
        mid_c.append(put(G.at[block, 0, :, lanes], G.at[block, 0, :, lanes], core))
    for copy in gat_y:
        copy.wait_recv()
    gat_c = put(G.at[:, 1, :, lanes], G.at[:, 1, :, lanes], core)

    up_x = [put(up_ref, up_all.at[gz], xpeer(d)) for d in (1, 3, 2)]
    proj_x = [put(proj_ref, proj_all.at[gz], xpeer(d)) for d in (1, 3, 2)]
    up_c = [put(up_ref, up_all.at[gz], core)]
    proj_c = [put(proj_ref, proj_all.at[gz], core)]
    for copy in attn_z:
        copy.wait_recv()

    def attn_rows(block):
        return pl.ds(pl.multiple_of(block * toks, toks), toks)

    own = attn_all.at[attn_rows(gz), :]
    attn_x = [put(own, own, xpeer(d)) for d in (1, 3, 2)]
    attn_c = [put(own, own, core)]

    for copy in mid_c:
        copy.wait_recv()
    gat_c.wait_recv()

    near = a < 4
    place = jnp.where(near, a, 7 - a)
    inner = {"gx": jnp.where(near, a + 1, a - 1)}
    outer = {"gx": jnp.clip(jnp.where(near, a - 1, a + 1), 0, 7)}
    lag = 4 - place

    def rs_copy(m):
        return pltpu.make_async_remote_copy(
            part.at[m], from_outer.at[m], rs_s.at[m], rs_r.at[m],
            device_id=inner, device_id_type=MESH)

    def xm_copy(m):
        return pltpu.make_async_remote_copy(
            part.at[m], from_mid.at[m], xm_s.at[m], xm_r.at[m],
            device_id=inner, device_id_type=MESH)

    def ag_copy(t, s):
        return pltpu.make_async_remote_copy(
            H.at[t, s], H.at[t, s], ag_s.at[t, s], ag_r.at[t, s],
            device_id=outer, device_id_type=MESH)

    def dp_same(k):
        t = lax.rem(x + k, 4)
        return pltpu.make_async_remote_copy(
            H.at[t, 1, :, lanes], HG.at[gz], dp_s.at[k, 0], dp_r.at[k, 0],
            device_id={"gz": t * 2 + c}, device_id_type=MESH)

    def dp_other(k):
        t = lax.rem(x + k, 4)
        return pltpu.make_async_remote_copy(
            H.at[t, 1, :, other_lanes], HG.at[gz], dp_s.at[k, 1], dp_r.at[k, 1],
            device_id={"gz": t * 2 + 1 - c}, device_id_type=MESH)

    def line_step(i, carry):
        @pl.when(i < 4)
        def _():
            t = lax.rem(x + i, 4)
            for s in range(2):
                m = i * 2 + s
                weight = up_ref if s == 0 else down_ref
                term = dot(weight[...], G[t, s], (1, 0))

                @pl.when(place == 0)
                def _():
                    part[m] = term.astype(BF16)

                @pl.when(place > 0)
                def _():
                    rs_copy(m).wait_recv()
                    part[m] = (term + from_outer[m].astype(F32)).astype(BF16)

                @pl.when(place < 3)
                def _():
                    rs_copy(m).start()

                @pl.when(place == 3)
                def _():
                    xm_copy(m).start()

        k = i - lag

        @pl.when((k >= 0) & (k < 4))
        def _():
            t = lax.rem(x + k, 4)

            @pl.when(place == 3)
            def _():
                xm_copy(2 * k).wait_recv()
                xm_copy(2 * k + 1).wait_recv()

                def rows_step(r, carry):
                    rows = pl.ds(pl.multiple_of(r * 32, 32), 32)
                    pre = part[2 * k, rows, :].astype(F32) + from_mid[2 * k, rows, :].astype(F32)
                    grad = part[2 * k + 1, rows, :].astype(F32) + from_mid[2 * k + 1, rows, :].astype(F32)
                    value, slope = gelu_pair(pre)
                    H[t, 0, rows, :] = value.astype(BF16)
                    H[t, 1, rows, :] = (grad * slope).astype(BF16)
                    return carry

                lax.fori_loop(0, units // 32, rows_step, 0)
                ag_copy(t, 1).start()
                ag_copy(t, 0).start()

            @pl.when(place < 3)
            def _():
                ag_copy(t, 1).wait_recv()

                @pl.when(place > 0)
                def _():
                    ag_copy(t, 1).start()

            @pl.when(k == 0)
            def _():
                HG[gz] = H[t, 1, :, lanes]

            @pl.when(k > 0)
            def _():
                dp_same(k).start()

            dp_other(k).start()

            @pl.when(place < 3)
            def _():
                ag_copy(t, 0).wait_recv()

                @pl.when(place > 0)
                def _():
                    ag_copy(t, 0).start()

        return carry

    lax.fori_loop(0, 8, line_step, 0)

    def hand_over(copies, ref_of, held):
        for copy, d in zip(copies, (1, 3, 2)):
            copy.wait_recv()
            block = lax.rem(x - d + 4, 4) * 2 + c
            held.append(put(ref_of(block), ref_of(block), core))

    hand_over(up_x, lambda block: up_all.at[block], up_c)
    hand_over(proj_x, lambda block: proj_all.at[block], proj_c)
    hand_over(attn_x, lambda block: attn_all.at[attn_rows(block), :], attn_c)

    for k in range(4):
        if k:
            dp_same(k).wait_recv()
        dp_other(k).wait_recv()
    for copy in up_c:
        copy.wait_recv()

    back[...] = dot(HG[0], up_all[0], (0, 0))

    def back_step(g, carry):
        back[...] += dot(HG[g], up_all[g], (0, 0))
        return carry

    lax.fori_loop(1, 8, back_step, 0)
    total_t = back[...].T
    back_send[...] = total_t.astype(BF16)
    y_rows_of = lambda d: pl.ds(pl.multiple_of(lax.rem(y + d, 4) * 2 * feats, 32), 2 * feats)
    y_sum = [put(back_send.at[y_rows_of(d), :], yr.at[d - 1], ypeer(d)) for d in (1, 3, 2)]

    def grad_weight(s, g, out):
        acc[...] = dot(H[0, s], G[0, g], (1, 1))

        def step(t, carry):
            acc[...] += dot(H[t, s], G[t, g], (1, 1))
            return carry

        lax.fori_loop(1, 4, step, 0)
        out[...] = (acc[...] * factor).astype(BF16)

    grad_weight(1, 0, gup_ref)
    for copy in y_sum:
        copy.wait_recv()
    total = back_send[y_rows, :].astype(F32)
    for d in range(3):
        total = total + yr[d].astype(F32)
    tot[...] = total
    tot[h_rows, :] += og_t[...]
    t_send[...] = tot[...].astype(BF16)
    h_sum = put(t_send, hr, hpeer)
    grad_weight(0, 1, gdown_ref)
    gate_copy.wait_recv()
    h_sum.wait_recv()
    total = tot[...] + hr[...].astype(F32)
    GM[y_rows, :] = (total * gates[...].astype(F32)).astype(BF16)
    gm_y = [put(GM.at[y_rows, :], GM.at[y_rows, :], ypeer(d)) for d in (1, 3, 2)]
    tot[...] = total
    gmid_ref[...] = tot[h_rows, :].T.astype(BF16)
    for copy in proj_c:
        copy.wait_recv()
    for copy in gm_y:
        copy.wait_recv()

    gp_copies = []
    feat_rows = lambda g: pl.ds(pl.multiple_of(g * feats, 16), feats)
    gz_lanes = pl.ds(pl.multiple_of(gz * toks, toks), toks)
    for d in range(1, 8):
        target = lax.rem(gz + d, 8)
        gp_copies.append(put(GM.at[feat_rows(target), :], GP.at[:, gz_lanes], gzpeer(d)))
    GP[:, gz_lanes] = GM[feat_rows(gz), :]
    back[...] = dot(GM[feat_rows(0), :], proj_all[0], (0, 0))

    def proj_step(g, carry):
        back[...] += dot(GM[feat_rows(g), :], proj_all[g], (0, 0))
        return carry

    lax.fori_loop(1, 8, proj_step, 0)
    ap[...] = back[...].astype(BF16).reshape(ap.shape)
    ar_copies = [put(ap.at[lax.rem(a + d, 8)], ar.at[d - 1], gxpeer(d)) for d in (4, 3, 5, 2, 6, 1, 7)]
    for copy in attn_c:
        copy.wait_recv()
    for copy in gp_copies:
        copy.wait_recv()
    gproj_ref[...] = (dot(GP[...], attn_all[...], (1, 0)) * factor).astype(BF16)
    for copy in ar_copies:
        copy.wait_recv()
    total = ap[a].astype(F32)
    for d in range(7):
        total = total + ar[d].astype(F32)
    gattn_ref[...] = total.astype(BF16)

    for copy in sent:
        copy.wait_send()

    def drain(m, carry):
        @pl.when(place < 3)
        def _():
            rs_copy(m).wait_send()

        @pl.when(place == 3)
        def _():
            xm_copy(m).wait_send()

        @pl.when(place > 0)
        def _():
            ag_copy(m // 2, lax.rem(m, 2)).wait_send()

        return carry

    lax.fori_loop(0, 8, drain, 0)
    for k in range(4):
        if k:
            dp_same(k).wait_send()
        dp_other(k).wait_send()


def per_device(
    mid_stream, out_grad, attn_values, attn_gate, ffn_gate, up_weight, down_weight, proj_weight
):
    toks, feats = mid_stream.shape
    units, wide = up_weight.shape
    tok_total = toks * lax.axis_size("gz")
    factor = float(tok_total) ** (-0.5)
    vmem = pl.BlockSpec(memory_space=pltpu.VMEM)
    pair = 2 * toks
    dma = pltpu.SemaphoreType.DMA
    scratch = [
        pltpu.VMEM((4, 2, wide, pair), BF16),
        pltpu.VMEM((8, units, pair), BF16),
        pltpu.VMEM((8, units, pair), BF16),
        pltpu.VMEM((8, units, pair), BF16),
        pltpu.VMEM((4, 2, units, pair), BF16),
        pltpu.VMEM((8, units, wide), BF16),
        pltpu.VMEM((8, feats, wide), BF16),
        pltpu.VMEM((tok_total, wide), BF16),
        pltpu.VMEM((2 * feats, toks), BF16),
        pltpu.VMEM((feats, toks), F32),
        pltpu.VMEM((8, units, toks), BF16),
        pltpu.VMEM((toks, wide), F32),
        pltpu.VMEM((2 * feats, toks), F32),
        pltpu.VMEM((wide, toks), BF16),
        pltpu.VMEM((3, 2 * feats, toks), BF16),
        pltpu.VMEM((2 * feats, toks), BF16),
        pltpu.VMEM((2 * feats, toks), BF16),
        pltpu.VMEM((wide, toks), BF16),
        pltpu.VMEM((feats, tok_total), BF16),
        pltpu.VMEM((8, toks // 8, wide), BF16),
        pltpu.VMEM((7, toks // 8, wide), BF16),
        pltpu.VMEM((units, wide), F32),
        dma((8,)), dma((8,)), dma((8,)), dma((8,)), dma((4, 2)), dma((4, 2)),
        dma((4, 2)), dma((4, 2)), dma((72,)), dma((72,)),
    ]
    shape = jax.ShapeDtypeStruct
    return pl.pallas_call(
        functools.partial(kernel, factor),
        out_shape=(
            shape((toks, feats), BF16),
            shape((attn_values.shape[0], wide), BF16),
            shape((feats, wide), BF16),
            shape((units, wide), BF16),
            shape((units, wide), BF16),
        ),
        in_specs=[vmem] * 8,
        out_specs=(vmem,) * 5,
        scratch_shapes=scratch,
        compiler_params=pltpu.CompilerParams(
            collective_id=0, has_side_effects=True, vmem_limit_bytes=48 * 1024 * 1024
        ),
        cost_estimate=pl.CostEstimate(flops=2_500_000_000, bytes_accessed=3_000_000, transcendentals=0),
        name="block_backward",
    )(
        mid_stream, out_grad, attn_values, attn_gate.reshape(1, feats), ffn_gate.reshape(1, feats),
        up_weight, down_weight, proj_weight,
    )


def solution(mesh):
    return jax.shard_map(
        per_device,
        mesh=mesh,
        in_specs=(
            P("gz", ("gx", "gy")),
            P("gz", ("gx", "gy")),
            P(("gz", "gx"), "gy"),
            P(("gx", "gy")),
            P(("gx", "gy")),
            P(("gy", "gz"), "gx"),
            P(("gy", "gz"), "gx"),
            P(("gx", "gz"), "gy"),
        ),
        out_specs=(
            P("gz", ("gx", "gy")),
            P(("gz", "gx"), "gy"),
            P(("gx", "gz"), "gy"),
            P(("gy", "gz"), "gx"),
            P(("gy", "gz"), "gx"),
        ),
        check_vma=False,
    )
```

time: 539 us -> 146 us (0.27)
  the two profiles are of different devices: /device:TPU:4 before, /device:TPU:2 now
where the time goes in v1:
time: 146 us
  Pallas kernels  137 us (94%)
  local copies, waits for them, and re-layouts  8.01 us (5%)
    pallas_call x1, Pallas kernels, per_device(): pl.pallas_call(functools.partial(kernel, factor), out_shape=(shape((toks,...  137 us
    unnamed x20, local copies, waits for them, and re-layouts  7.3 us

profile of v1, /device:TPU:2, one launch (start us, length us, event | category | flops | bytes accessed | tf_op | source)
XLA Modules:
  0.0 145.7 jit_solution(13460112171588265595)
XLA Ops:
  0.6 0.0 copy-start.6
  0.6 0.9 copy.13.mid_ref
  1.5 0.0 copy-done.6
  1.5 0.0 copy-start.3
  1.5 0.0 copy-start.4
  1.5 0.0 copy-start.5
  1.5 0.1 copy.14.out_ref
  1.7 0.6 copy-done.3
  2.3 0.0 copy-done.4
  2.3 0.0 copy-done.5
  2.3 0.0 copy-start
  2.3 1.0 copy-done
  3.3 0.0 copy-start.1
  3.3 1.0 copy-done.1
  4.3 0.0 copy-start.2
  4.3 0.9 copy-done.2
  5.2 137.0 %block_backward.1 = (bf16[128,112]{1,0:T(8,128)(2,1)S(1)}, bf16[16,896]{1,0:T(8,128)(2,1)S(1)}, bf16[112,896]{1,0:T(8,128)(2,1)S(1)}, bf16[224,896]{1,0:T(8,128)(2,1)S(1)}, bf16[224,896]{1,0:T(8,128)(2,1)S(1)}) custom-call(bf16[128,112]{1,0:T(8,128)(2,1)S(1)} %copy.13.mid_ref, bf16[128,112]{1,0:T(8,128)(2,1)S(1)} %copy.14.out_ref, ...), custom_call_target="tpu_custom_call" | custom-call | flops 2500000000 | bytes 3000000 | tf_op jit(solution)/shard_map/block_backward/pallas_call | solution.py:406
  142.2 0.7 copy.15
  143.0 0.6 copy.20
  143.6 0.7 copy.21
  144.3 0.7 copy.22
  145.0 0.7 copy.23
Async XLA Ops:
  0.6 0.9 copy-start.6
  1.5 0.8 copy-start.3
  1.5 0.7 copy-start.4
  1.5 0.7 copy-start.5
  2.3 1.0 copy-start
  3.3 1.0 copy-start.1
  4.3 0.9 copy-start.2

commit v2 on v1

v2 whole, which is shorter than its diff:
```python
import functools

import jax
import jax.numpy as jnp
from jax import lax
from jax.experimental import pallas as pl
from jax.experimental.pallas import tpu as pltpu
from jax.sharding import PartitionSpec as P

MESH = pl.DeviceIdType.MESH
BF16, F32 = jnp.bfloat16, jnp.float32
root_two_pi = 0.7978845608028654
cubic_term = 0.044715


def dot(former, latter, contract):
    return lax.dot_general(
        former, latter, ((contract[:1], contract[1:]), ((), ())), preferred_element_type=F32
    )


def gelu_pair(values):
    square = values * values
    tangent = jnp.tanh(root_two_pi * (values + cubic_term * values * square))
    half = 0.5 * (1.0 + tangent)
    slope = half + 0.5 * values * (1.0 - tangent * tangent) * root_two_pi * (
        1.0 + 3.0 * cubic_term * square
    )
    return values * half, slope


def kernel(
    factor,
    mid_in, out_in, attn_in, agate_in, fgate_in, up_in, down_in, proj_in,
    gmid_ref, gattn_ref, gproj_ref, gup_ref, gdown_ref,
    G, term, part, from_outer, from_mid, H, up_all, down_own, proj_all, attn_all, gates, og, ag_row, fg_row,
    HG, back, tot, back_send, yr, t_send, hr, GM, GP, ap, ar, acc,
    rs_s, rs_r, xm_s, xm_r, ag_s, ag_r, dp_s, dp_r, send_sems, recv_sems, local_sems,
):
    feats, toks = mid_in.shape
    units = up_in.shape[0]
    units_order = ((0, 0), (1, 0), (1, 1), (2, 0), (2, 1), (3, 0), (3, 1), (0, 1))
    steps = len(units_order)
    lags = (steps, 6, 4, 1)
    a = lax.axis_index("gx")
    gy = lax.axis_index("gy")
    gz = lax.axis_index("gz")
    x, c = gz // 2, lax.rem(gz, 2)
    y, h = gy // 2, lax.rem(gy, 2)

    def xpeer(d):
        return {"gz": lax.rem(x + d, 4) * 2 + c}

    def ypeer(d):
        return {"gy": lax.rem(y + d, 4) * 2 + h}

    core = {"gz": x * 2 + 1 - c}
    hpeer = {"gy": y * 2 + 1 - h}

    def gxpeer(d):
        return {"gx": lax.rem(a + d, 8)}

    def gzpeer(d):
        return {"gz": lax.rem(gz + d, 8)}

    barrier = pltpu.get_barrier_semaphore()
    peers = [gzpeer(d) for d in range(1, 8)] + [gxpeer(d) for d in range(1, 8)]
    peers += [ypeer(d) for d in range(1, 4)] + [hpeer]
    for peer in peers:
        pl.semaphore_signal(barrier, inc=1, device_id=peer, device_id_type=MESH)

    sent, open_recv = [], []
    count = [0]

    def put(src, dst, peer):
        index = count[0]
        count[0] += 1
        copy = pltpu.make_async_remote_copy(
            src, dst, send_sems.at[index], recv_sems.at[index],
            device_id=peer, device_id_type=MESH,
        )
        copy.start()
        sent.append(copy)
        open_recv.append(copy)
        return copy

    def arrive(copy):
        copy.wait_recv()
        open_recv[:] = [other for other in open_recv if other is not copy]

    def finish(line):
        for copy in open_recv:
            copy.wait_recv()
        for copy in sent:
            copy.wait_send()
        if not line:
            return

        for u in range(steps):
            for s in range(2):
                @pl.when(place < 3)
                def _():
                    rs_copy(s, u).wait_send()

                @pl.when(place == 3)
                def _():
                    xm_copy(s, u).wait_send()

                @pl.when(place > 0)
                def _():
                    ag_copy(s, u).wait_send()

        drain_spread(lambda copy: copy.wait_send())

    own_rows = pl.ds(pl.multiple_of(gy * feats, 16), feats)
    y_rows = pl.ds(pl.multiple_of(y * 2 * feats, 32), 2 * feats)
    h_rows = pl.ds(pl.multiple_of(h * feats, 16), feats)

    partner_rows = pl.ds(pl.multiple_of((y * 2 + 1 - h) * feats, 16), feats)
    attn_row = pl.ds(pl.multiple_of((gz * 8 + a) * 16, 16), 16)

    loads = [
        pltpu.make_async_copy(src, dst, local_sems.at[n])
        for n, (src, dst) in enumerate((
            (mid_in, G.at[x, c, 0, own_rows, :]),
            (out_in, og),
            (fgate_in, fg_row),
            (agate_in, ag_row),
            (up_in, up_all.at[gz]),
            (down_in, down_own),
            (proj_in, proj_all.at[gz]),
            (attn_in, attn_all.at[attn_row, :]),
        ))
    ]
    for load in loads:
        load.start()
    for load in loads[:4]:
        load.wait()

    def gate_columns(row):
        return jnp.broadcast_to(row[...].astype(F32), (toks, feats)).T

    G[x, c, 1, own_rows, :] = (og[...].astype(F32) * gate_columns(fg_row)).astype(BF16)
    gates[h_rows, :] = gate_columns(ag_row).astype(BF16)
    for load in loads[4:]:
        load.wait()

    pl.semaphore_wait(barrier, len(peers))

    near_first = (2, 1, 3)

    def block_from(d):
        return lax.rem(x - d + 4, 4)

    h_copy = put(G.at[x, c, :, own_rows, :], G.at[x, c, :, own_rows, :], hpeer)
    own_y = [put(G.at[x, c, :, own_rows, :], G.at[x, c, :, own_rows, :], ypeer(d)) for d in near_first]
    gat_x = [[put(G.at[x, c, 1, own_rows, :], G.at[x, c, 1, own_rows, :], xpeer(d))] for d in near_first]
    arrive(h_copy)
    own_y += [
        put(G.at[x, c, :, partner_rows, :], G.at[x, c, :, partner_rows, :], ypeer(d)) for d in near_first
    ]
    for copies, d in zip(gat_x, near_first):
        copies.append(put(G.at[x, c, 1, partner_rows, :], G.at[x, c, 1, partner_rows, :], xpeer(d)))
    own_attn = attn_all.at[attn_row, :]
    attn_z = [put(own_attn, own_attn, gxpeer(d)) for d in range(1, 8)]
    gate_copy = put(gates.at[h_rows, :], gates.at[h_rows, :], hpeer)
    for copy in own_y:
        arrive(copy)
    own_c = put(G.at[x, c], G.at[x, c], core)
    mid_x = [put(G.at[x, c, 0], G.at[x, c, 0], xpeer(d)) for d in near_first]
    gat_y = []
    for copies, d in zip(gat_x, near_first):
        for copy in copies:
            arrive(copy)
        rows = G.at[block_from(d), c, 1, y_rows, :]
        gat_y.append([put(rows, rows, ypeer(e)) for e in near_first])

    def acquire(n):
        block = block_from(near_first[n])
        arrive(mid_x[n])
        mid_rows, gat_rows = G.at[block, c, 0], G.at[block, c, 1]
        halves = [put(mid_rows, mid_rows, core)]
        for copy in gat_y[n]:
            arrive(copy)
        halves.append(put(gat_rows, gat_rows, core))
        for copy in halves:
            arrive(copy)

    def attn_rows(block):
        return pl.ds(pl.multiple_of(block * toks, toks), toks)

    def hand_over(copies, ref_of, held):
        for copy, d in zip(copies, near_first):
            arrive(copy)
            block = block_from(d) * 2 + c
            held.append(put(ref_of(block), ref_of(block), core))

    near = a < 4
    place = jnp.where(near, a, 7 - a)
    inner = {"gx": jnp.where(near, a + 1, a - 1)}
    outer = {"gx": jnp.clip(jnp.where(near, a - 1, a + 1), 0, 7)}
    def block_of(k):
        return lax.rem(x + (0, 2, 3, 1)[k], 4)

    def rs_copy(s, u):
        return pltpu.make_async_remote_copy(
            part.at[u, s], from_outer.at[u, s], rs_s.at[u, s], rs_r.at[u, s],
            device_id=inner, device_id_type=MESH)

    def xm_copy(s, u):
        return pltpu.make_async_remote_copy(
            part.at[u, s], from_mid.at[u, s], xm_s.at[u, s], xm_r.at[u, s],
            device_id=inner, device_id_type=MESH)

    def held_at(u, s):
        k, kind = units_order[u]
        return block_of(k), half_of(kind), s

    def half_of(kind):
        return 1 - c if kind else c

    def ag_copy(s, u):
        place_held = H.at[held_at(u, s)]
        return pltpu.make_async_remote_copy(
            place_held, place_held, ag_s.at[u, s], ag_r.at[u, s],
            device_id=outer, device_id_type=MESH)

    def dp_copy(k, kind):
        t, half = block_of(k), half_of(kind)
        return pltpu.make_async_remote_copy(
            H.at[t, half, 1], HG.at[gz], dp_s.at[k, kind], dp_r.at[k, kind],
            device_id={"gz": t * 2 + half}, device_id_type=MESH)

    def spread(u):
        k, kind = units_order[u]
        if k or kind:
            dp_copy(k, kind).start()
        else:
            HG[gz] = H[x, c, 1]

    def products(u):
        t, half, _ = held_at(u, 0)
        term[u % 2, 0] = dot(up_all[gz], G[t, half, 0], (1, 0))
        term[u % 2, 1] = dot(down_own[...], G[t, half, 1], (1, 0))

    def reduce_step(u):
        kind = u % 2
        for s in range(2):
            @pl.when(place == 0)
            def _():
                part[u, s] = term[kind, s].astype(BF16)

            @pl.when(place > 0)
            def _():
                rs_copy(s, u).wait_recv()
                part[u, s] = (term[kind, s] + from_outer[u, s].astype(F32)).astype(BF16)

            @pl.when(place < 3)
            def _():
                rs_copy(s, u).start()

            @pl.when(place == 3)
            def _():
                xm_copy(s, u).start()

    def turn_step(u):
        xm_copy(0, u).wait_recv()
        xm_copy(1, u).wait_recv()
        value, slope = gelu_pair(part[u, 0].astype(F32) + from_mid[u, 0].astype(F32))
        H[held_at(u, 1)] = ((part[u, 1].astype(F32) + from_mid[u, 1].astype(F32)) * slope).astype(BF16)
        ag_copy(1, u).start()
        H[held_at(u, 0)] = value.astype(BF16)
        ag_copy(0, u).start()
        spread(u)

    def pass_on(u):
        for s in (1, 0):
            ag_copy(s, u).wait_recv()

            @pl.when(place > 0)
            def _():
                ag_copy(s, u).start()

            if s:
                spread(u)

    up_x = []
    attn_block = attn_all.at[attn_rows(gz), :]
    own_up, own_proj = up_all.at[gz], proj_all.at[gz]
    for u in range(2 * steps):
        if u < steps:
            k, kind = units_order[u]
            if k == 0 and kind:
                arrive(own_c)
            if k and kind == 0:
                acquire(k - 1)
                if k == 2:
                    up_x += [put(own_up, own_up, xpeer(d)) for d in near_first]
            products(u)
            reduce_step(u)
        if u == 11:
            up_c = [put(own_up, own_up, core)]
            hand_over(up_x, lambda block: up_all.at[block], up_c)
        for where, lag in enumerate(lags):
            if lag <= u < lag + steps:
                @pl.when(place == where)
                def _():
                    (turn_step if where == 3 else pass_on)(u - lag)

    proj_x = [put(own_proj, own_proj, xpeer(d)) for d in near_first]
    proj_c = [put(own_proj, own_proj, core)]
    for copy in attn_z:
        arrive(copy)
    attn_x = [put(attn_block, attn_block, xpeer(d)) for d in near_first]
    attn_c = [put(attn_block, attn_block, core)]

    def drain_spread(act):
        for k in range(4):
            for kind in range(2):
                if k or kind:
                    act(dp_copy(k, kind))

    for copy in up_c:
        arrive(copy)
    for u, (k, kind) in enumerate(units_order):
        if u:
            dp_copy(k, kind).wait_recv()
        source = lax.rem(x + (0, 2, 1, 3)[k], 4) * 2 + half_of(kind)
        product = dot(HG[source], up_all[source], (0, 0))
        back[...] = back[...] + product if u else product
    total_t = back[...].T
    back_send[...] = total_t.astype(BF16)
    y_rows_of = lambda d: pl.ds(pl.multiple_of(lax.rem(y + d, 4) * 2 * feats, 32), 2 * feats)
    y_sum = [put(back_send.at[y_rows_of(d), :], yr.at[d - 1], ypeer(d)) for d in (1, 3, 2)]

    def joined(ref, t, s):
        return jnp.concatenate([ref[t, 0, s], ref[t, 1, s]], 1)

    def grad_weight(s, g, out):
        acc[...] = dot(joined(H, 0, s), joined(G, 0, g), (1, 1))

        def step(t, carry):
            acc[...] += dot(joined(H, t, s), joined(G, t, g), (1, 1))
            return carry

        lax.fori_loop(1, 4, step, 0)
        out[...] = (acc[...] * factor).astype(BF16)

    grad_weight(1, 0, gup_ref)
    for copy in y_sum:
        arrive(copy)
    total = back_send[y_rows, :].astype(F32)
    for d in range(3):
        total = total + yr[d].astype(F32)
    tot[...] = total
    tot[h_rows, :] += og[...].astype(F32)
    t_send[...] = tot[...].astype(BF16)
    h_sum = put(t_send, hr, hpeer)
    hand_over(proj_x, lambda block: proj_all.at[block], proj_c)
    grad_weight(0, 1, gdown_ref)
    arrive(gate_copy)
    arrive(h_sum)
    total = tot[...] + hr[...].astype(F32)
    GM[y_rows, :] = (total * gates[...].astype(F32)).astype(BF16)
    gm_y = [put(GM.at[y_rows, :], GM.at[y_rows, :], ypeer(d)) for d in (1, 3, 2)]
    tot[...] = total
    gmid_ref[...] = tot[h_rows, :].astype(BF16)
    for copy in proj_c:
        arrive(copy)

    def feat_rows(g):
        return pl.ds(pl.multiple_of(g * feats, 16), feats)

    def proj_part(pair):
        return sum(dot(GM[feat_rows(pair * 2 + n), :], proj_all[pair * 2 + n], (0, 0)) for n in range(2))

    back[...] = proj_part(y)
    for copy, d in zip(gm_y, (1, 3, 2)):
        arrive(copy)
        back[...] += proj_part(lax.rem(y - d + 4, 4))

    ap[...] = back[...].astype(BF16).reshape(ap.shape)
    ar_copies = [put(ap.at[lax.rem(a + d, 8)], ar.at[d - 1], gxpeer(d)) for d in (4, 3, 5, 2, 6, 1, 7)]
    gp_copies = []
    for d in range(1, 8):
        gp_copies.append(put(GM.at[feat_rows(lax.rem(gz + d, 8)), :], GP.at[gz], gzpeer(d)))
    GP[gz] = GM[feat_rows(gz), :]
    hand_over(attn_x, lambda block: attn_all.at[attn_rows(block), :], attn_c)
    for copy in attn_c:
        arrive(copy)
    for copy in gp_copies:
        arrive(copy)
    gproj_ref[...] = (dot(jnp.concatenate([GP[g] for g in range(8)], 1), attn_all[...], (1, 0)) * factor).astype(BF16)
    for copy in ar_copies:
        arrive(copy)
    total = ap[a].astype(F32)
    for d in range(7):
        total = total + ar[d].astype(F32)
    gattn_ref[...] = total.astype(BF16)

    finish(True)


def write_out(*refs):
    sources, targets, sems = refs[:5], refs[5:10], refs[10]
    copies = [
        pltpu.make_async_copy(source, target, sems.at[n])
        for n, (source, target) in enumerate(zip(sources, targets))
    ]
    for copy in copies:
        copy.start()
    for copy in copies:
        copy.wait()


def per_device(
    mid_stream, out_grad, attn_values, attn_gate, ffn_gate, up_weight, down_weight, proj_weight
):
    toks, feats = mid_stream.shape
    units, wide = up_weight.shape
    tok_total = toks * lax.axis_size("gz")
    factor = float(tok_total) ** (-0.5)
    vmem = pl.BlockSpec(memory_space=pltpu.VMEM)
    anywhere = pl.BlockSpec(memory_space=pl.ANY)
    dma = pltpu.SemaphoreType.DMA
    scratch = [
        pltpu.VMEM((4, 2, 2, wide, toks), BF16),
        pltpu.VMEM((2, 2, units, toks), F32),
        pltpu.VMEM((8, 2, units, toks), BF16),
        pltpu.VMEM((8, 2, units, toks), BF16),
        pltpu.VMEM((8, 2, units, toks), BF16),
        pltpu.VMEM((4, 2, 2, units, toks), BF16),
        pltpu.VMEM((8, units, wide), BF16),
        pltpu.VMEM((units, wide), BF16),
        pltpu.VMEM((8, feats, wide), BF16),
        pltpu.VMEM((tok_total, wide), BF16),
        pltpu.VMEM((2 * feats, toks), BF16),
        pltpu.VMEM((feats, toks), BF16),
        pltpu.VMEM((1, feats), BF16),
        pltpu.VMEM((1, feats), BF16),
        pltpu.VMEM((8, units, toks), BF16),
        pltpu.VMEM((toks, wide), F32),
        pltpu.VMEM((2 * feats, toks), F32),
        pltpu.VMEM((wide, toks), BF16),
        pltpu.VMEM((3, 2 * feats, toks), BF16),
        pltpu.VMEM((2 * feats, toks), BF16),
        pltpu.VMEM((2 * feats, toks), BF16),
        pltpu.VMEM((wide, toks), BF16),
        pltpu.VMEM((8, feats, toks), BF16),
        pltpu.VMEM((8, toks // 8, wide), BF16),
        pltpu.VMEM((7, toks // 8, wide), BF16),
        pltpu.VMEM((units, wide), F32),
        *[dma((8, 2))] * 6,
        dma((4, 2)), dma((4, 2)), dma((96,)), dma((96,)), dma((8,)),
    ]
    shape = jax.ShapeDtypeStruct
    shapes = (
        shape((feats, toks), BF16),
        shape((attn_values.shape[0], wide), BF16),
        shape((feats, wide), BF16),
        shape((units, wide), BF16),
        shape((units, wide), BF16),
    )
    results = pl.pallas_call(
        functools.partial(kernel, factor),
        out_shape=shapes,
        in_specs=[pl.BlockSpec(memory_space=pltpu.HBM)] * 8,
        out_specs=(vmem,) * 5,
        scratch_shapes=scratch,
        compiler_params=pltpu.CompilerParams(
            collective_id=0, has_side_effects=True, vmem_limit_bytes=63 * 1024 * 1024
        ),
        cost_estimate=pl.CostEstimate(flops=2_500_000_000, bytes_accessed=3_000_000, transcendentals=0),
        name="block_backward",
    )(
        mid_stream.T, out_grad.T, attn_values, attn_gate.reshape(1, feats), ffn_gate.reshape(1, feats),
        up_weight, down_weight, proj_weight,
    )
    grad_mid, *others = pl.pallas_call(
        write_out,
        out_shape=shapes,
        in_specs=[vmem] * 5,
        out_specs=(anywhere,) * 5,
        scratch_shapes=[dma((5,))],
        cost_estimate=pl.CostEstimate(flops=0, bytes_accessed=3_000_000, transcendentals=0),
        name="write_out",
    )(*results)
    return (grad_mid.T, *others)


def solution(mesh):
    return jax.shard_map(
        per_device,
        mesh=mesh,
        in_specs=(
            P("gz", ("gx", "gy")),
            P("gz", ("gx", "gy")),
            P(("gz", "gx"), "gy"),
            P(("gx", "gy")),
            P(("gx", "gy")),
            P(("gy", "gz"), "gx"),
            P(("gy", "gz"), "gx"),
            P(("gx", "gz"), "gy"),
        ),
        out_specs=(
            P("gz", ("gx", "gy")),
            P(("gz", "gx"), "gy"),
            P(("gx", "gz"), "gy"),
            P(("gy", "gz"), "gx"),
            P(("gy", "gz"), "gx"),
        ),
        check_vma=False,
    )
```

time: 146 us -> 121 us (0.83)
  Pallas kernels: 137 us -> 120 us
  local copies, waits for them, and re-layouts: 8.01 us -> 0 us
    pallas_call x1 -> x2, Pallas kernels: 137 us -> 120 us  [the longest x1 118 us: per_device(): pl.pallas_call(functools.partial(kernel, factor), out_shape=shapes, in_sp...]
    unnamed x20 -> x0, local copies, waits for them, and re-layouts: 7.3 us -> none
where the time goes in v2:
time: 121 us
  Pallas kernels  120 us (99%)
    pallas_call x1, Pallas kernels, per_device(): pl.pallas_call(functools.partial(kernel, factor), out_shape=shapes, in_sp...  118 us

profile of v2, /device:TPU:2, one launch (start us, length us, event | category | flops | bytes accessed | tf_op | source)
XLA Modules:
  0.0 120.6 jit_solution(4115449635575744510)
XLA Ops:
  0.6 117.7 %block_backward.1 = (bf16[112,128]{1,0:T(8,128)(2,1)}, bf16[16,896]{1,0:T(8,128)(2,1)}, bf16[112,896]{1,0:T(8,128)(2,1)}, bf16[224,896]{1,0:T(8,128)(2,1)}, bf16[224,896]{1,0:T(8,128)(2,1)}) custom-call(bf16[112,128]{1,0:T(8,128)(2,1)} %bitcast.5, bf16[112,128]{1,0:T(8,128)(2,1)} %bitcast.6, bf16[16,896]{1,0:T(8,128)(2,1)} %attn_in.1, ...), custom_call_target="tpu_custom_call" | custom-call | flops 2500000000 | bytes 3000000 | tf_op jit(solution)/shard_map/block_backward/pallas_call | solution.py:464
  118.3 2.3 %write_out.1 = (bf16[112,128]{1,0:T(8,128)(2,1)}, bf16[16,896]{1,0:T(8,128)(2,1)}, bf16[112,896]{1,0:T(8,128)(2,1)}, bf16[224,896]{1,0:T(8,128)(2,1)}, bf16[224,896]{1,0:T(8,128)(2,1)}) custom-call(bf16[112,128]{1,0:T(8,128)(2,1)} %get-tuple-element.15.refs_0_, bf16[16,896]{1,0:T(8,128)(2,1)} %get-tuple-element.16.refs_1_, ...), custom_call_target="tpu_custom_call" | custom-call | bytes 3000000 | tf_op jit(solution)/shard_map/write_out/pallas_call | solution.py:479

commit v3 on v2

--- a/solution.py
+++ b/solution.py
@@ -98,17 +98,18 @@
 
         for u in range(steps):
             for s in range(2):
-                @pl.when(place < 3)
-                def _():
-                    rs_copy(s, u).wait_send()
-
-                @pl.when(place == 3)
-                def _():
-                    xm_copy(s, u).wait_send()
-
-                @pl.when(place > 0)
-                def _():
-                    ag_copy(s, u).wait_send()
+                for r in range(pieces):
+                    @pl.when(place < 3)
+                    def _():
+                        rs_copy(s, u, r).wait_send()
+
+                    @pl.when(place == 3)
+                    def _():
+                        xm_copy(s, u, r).wait_send()
+
+                    @pl.when(place > 0)
+                    def _():
+                        ag_copy(s, u, r).wait_send()
 
         drain_spread(lambda copy: copy.wait_send())
 
@@ -202,15 +203,20 @@
     def block_of(k):
         return lax.rem(x + (0, 2, 3, 1)[k], 4)
 
-    def rs_copy(s, u):
+    def rs_copy(s, u, r):
         return pltpu.make_async_remote_copy(
-            part.at[u, s], from_outer.at[u, s], rs_s.at[u, s], rs_r.at[u, s],
+            part.at[u, s, rows_of(r)], from_outer.at[u, s, rows_of(r)], rs_s.at[u, s, r], rs_r.at[u, s, r],
             device_id=inner, device_id_type=MESH)
 
-    def xm_copy(s, u):
+    def xm_copy(s, u, r):
         return pltpu.make_async_remote_copy(
-            part.at[u, s], from_mid.at[u, s], xm_s.at[u, s], xm_r.at[u, s],
+            part.at[u, s, rows_of(r)], from_mid.at[u, s, rows_of(r)], xm_s.at[u, s, r], xm_r.at[u, s, r],
             device_id=inner, device_id_type=MESH)
+
+    pieces = rs_s.shape[2]
+
+    def rows_of(r):
+        return pl.ds(r * (units // pieces), units // pieces)
 
     def held_at(u, s):
         k, kind = units_order[u]
@@ -219,10 +225,11 @@
     def half_of(kind):
         return 1 - c if kind else c
 
-    def ag_copy(s, u):
-        place_held = H.at[held_at(u, s)]
+    def ag_copy(s, u, r):
+        t, half, _ = held_at(u, s)
+        rows = H.at[t, half, s, rows_of(r)]
         return pltpu.make_async_remote_copy(
-            place_held, place_held, ag_s.at[u, s], ag_r.at[u, s],
+            rows, rows, ag_s.at[u, s, r], ag_r.at[u, s, r],
             device_id=outer, device_id_type=MESH)
 
     def dp_copy(k, kind):
@@ -245,41 +252,49 @@
 
     def reduce_step(u):
         kind = u % 2
-        for s in range(2):
-            @pl.when(place == 0)
-            def _():
-                part[u, s] = term[kind, s].astype(BF16)
-
-            @pl.when(place > 0)
-            def _():
-                rs_copy(s, u).wait_recv()
-                part[u, s] = (term[kind, s] + from_outer[u, s].astype(F32)).astype(BF16)
-
-            @pl.when(place < 3)
-            def _():
-                rs_copy(s, u).start()
-
-            @pl.when(place == 3)
-            def _():
-                xm_copy(s, u).start()
+        for r in range(pieces):
+            rows = rows_of(r)
+            for s in range(2):
+                @pl.when(place == 0)
+                def _():
+                    part[u, s, rows] = term[kind, s, rows].astype(BF16)
+
+                @pl.when(place > 0)
+                def _():
+                    rs_copy(s, u, r).wait_recv()
+                    part[u, s, rows] = (term[kind, s, rows] + from_outer[u, s, rows].astype(F32)).astype(BF16)
+
+                @pl.when(place < 3)
+                def _():
+                    rs_copy(s, u, r).start()
+
+                @pl.when(place == 3)
+                def _():
+                    xm_copy(s, u, r).start()
 
     def turn_step(u):
-        xm_copy(0, u).wait_recv()
-        xm_copy(1, u).wait_recv()
-        value, slope = gelu_pair(part[u, 0].astype(F32) + from_mid[u, 0].astype(F32))
-        H[held_at(u, 1)] = ((part[u, 1].astype(F32) + from_mid[u, 1].astype(F32)) * slope).astype(BF16)
-        ag_copy(1, u).start()
-        H[held_at(u, 0)] = value.astype(BF16)
-        ag_copy(0, u).start()
+        t, half, _ = held_at(u, 0)
+        for r in range(pieces):
+            rows = rows_of(r)
+            xm_copy(0, u, r).wait_recv()
+            xm_copy(1, u, r).wait_recv()
+            value, slope = gelu_pair(part[u, 0, rows].astype(F32) + from_mid[u, 0, rows].astype(F32))
+            grad = part[u, 1, rows].astype(F32) + from_mid[u, 1, rows].astype(F32)
+            H[t, half, 1, rows] = (grad * slope).astype(BF16)
+            ag_copy(1, u, r).start()
+            H[t, half, 0, rows] = value.astype(BF16)
+        for r in range(pieces):
+            ag_copy(0, u, r).start()
         spread(u)
 
     def pass_on(u):
         for s in (1, 0):
-            ag_copy(s, u).wait_recv()
-
-            @pl.when(place > 0)
-            def _():
-                ag_copy(s, u).start()
+            for r in range(pieces):
+                ag_copy(s, u, r).wait_recv()
+
+                @pl.when(place > 0)
+                def _():
+                    ag_copy(s, u, r).start()
 
             if s:
                 spread(u)
@@ -294,7 +309,7 @@
                 arrive(own_c)
             if k and kind == 0:
                 acquire(k - 1)
-                if k == 2:
+                if k == 1:
                     up_x += [put(own_up, own_up, xpeer(d)) for d in near_first]
             products(u)
             reduce_step(u)
@@ -330,8 +345,15 @@
         back[...] = back[...] + product if u else product
     total_t = back[...].T
     back_send[...] = total_t.astype(BF16)
-    y_rows_of = lambda d: pl.ds(pl.multiple_of(lax.rem(y + d, 4) * 2 * feats, 32), 2 * feats)
-    y_sum = [put(back_send.at[y_rows_of(d), :], yr.at[d - 1], ypeer(d)) for d in (1, 3, 2)]
+    def feat_rows(g):
+        return pl.ds(pl.multiple_of(g * feats, 16), feats)
+
+    def y_block(d, n):
+        return feat_rows(lax.rem(y + d, 4) * 2 + n)
+
+    y_sum = [
+        [put(back_send.at[y_block(d, n), :], yr.at[n, d - 1], ypeer(d)) for d in (1, 3, 2)] for n in range(2)
+    ]
 
     def joined(ref, t, s):
         return jnp.concatenate([ref[t, 0, s], ref[t, 1, s]], 1)
@@ -346,38 +368,38 @@
         lax.fori_loop(1, 4, step, 0)
         out[...] = (acc[...] * factor).astype(BF16)
 
+    h_sum, gm_y = [], []
+    for n in range(2):
+        for copy in y_sum[n]:
+            arrive(copy)
+        total = back_send[y_block(0, n), :].astype(F32) + jnp.where(h == n, 1.0, 0.0) * og[...].astype(F32)
+        for d in range(3):
+            total = total + yr[n, d].astype(F32)
+        tot[n] = total
+        t_send[n] = total.astype(BF16)
+        h_sum.append(put(t_send.at[n], hr.at[n], hpeer))
     grad_weight(1, 0, gup_ref)
-    for copy in y_sum:
-        arrive(copy)
-    total = back_send[y_rows, :].astype(F32)
-    for d in range(3):
-        total = total + yr[d].astype(F32)
-    tot[...] = total
-    tot[h_rows, :] += og[...].astype(F32)
-    t_send[...] = tot[...].astype(BF16)
-    h_sum = put(t_send, hr, hpeer)
     hand_over(proj_x, lambda block: proj_all.at[block], proj_c)
     grad_weight(0, 1, gdown_ref)
     arrive(gate_copy)
-    arrive(h_sum)
-    total = tot[...] + hr[...].astype(F32)
-    GM[y_rows, :] = (total * gates[...].astype(F32)).astype(BF16)
-    gm_y = [put(GM.at[y_rows, :], GM.at[y_rows, :], ypeer(d)) for d in (1, 3, 2)]
-    tot[...] = total
-    gmid_ref[...] = tot[h_rows, :].astype(BF16)
+    for n in range(2):
+        arrive(h_sum[n])
+        tot[n] += hr[n].astype(F32)
+        block = y_block(0, n)
+        GM[block, :] = (tot[n] * gates[pl.ds(n * feats, feats), :].astype(F32)).astype(BF16)
+        gm_y.append([put(GM.at[block, :], GM.at[block, :], ypeer(d)) for d in (1, 3, 2)])
+    gmid_ref[...] = tot[h].astype(BF16)
     for copy in proj_c:
         arrive(copy)
 
-    def feat_rows(g):
-        return pl.ds(pl.multiple_of(g * feats, 16), feats)
-
-    def proj_part(pair):
-        return sum(dot(GM[feat_rows(pair * 2 + n), :], proj_all[pair * 2 + n], (0, 0)) for n in range(2))
-
-    back[...] = proj_part(y)
-    for copy, d in zip(gm_y, (1, 3, 2)):
-        arrive(copy)
-        back[...] += proj_part(lax.rem(y - d + 4, 4))
+    def proj_part(g):
+        return dot(GM[feat_rows(g), :], proj_all[g], (0, 0))
+
+    back[...] = proj_part(y * 2) + proj_part(y * 2 + 1)
+    for n in range(2):
+        for copy, d in zip(gm_y[n], (1, 3, 2)):
+            arrive(copy)
+            back[...] += proj_part(lax.rem(y - d + 4, 4) * 2 + n)
 
     ap[...] = back[...].astype(BF16).reshape(ap.shape)
     ar_copies = [put(ap.at[lax.rem(a + d, 8)], ar.at[d - 1], gxpeer(d)) for d in (4, 3, 5, 2, 6, 1, 7)]
@@ -423,6 +445,7 @@
     vmem = pl.BlockSpec(memory_space=pltpu.VMEM)
     anywhere = pl.BlockSpec(memory_space=pl.ANY)
     dma = pltpu.SemaphoreType.DMA
+    pieces = 2
     scratch = [
         pltpu.VMEM((4, 2, 2, wide, toks), BF16),
         pltpu.VMEM((2, 2, units, toks), F32),
@@ -440,18 +463,18 @@
         pltpu.VMEM((1, feats), BF16),
         pltpu.VMEM((8, units, toks), BF16),
         pltpu.VMEM((toks, wide), F32),
-        pltpu.VMEM((2 * feats, toks), F32),
+        pltpu.VMEM((2, feats, toks), F32),
         pltpu.VMEM((wide, toks), BF16),
-        pltpu.VMEM((3, 2 * feats, toks), BF16),
-        pltpu.VMEM((2 * feats, toks), BF16),
-        pltpu.VMEM((2 * feats, toks), BF16),
+        pltpu.VMEM((2, 3, feats, toks), BF16),
+        pltpu.VMEM((2, feats, toks), BF16),
+        pltpu.VMEM((2, feats, toks), BF16),
         pltpu.VMEM((wide, toks), BF16),
         pltpu.VMEM((8, feats, toks), BF16),
         pltpu.VMEM((8, toks // 8, wide), BF16),
         pltpu.VMEM((7, toks // 8, wide), BF16),
         pltpu.VMEM((units, wide), F32),
-        *[dma((8, 2))] * 6,
-        dma((4, 2)), dma((4, 2)), dma((96,)), dma((96,)), dma((8,)),
+        *[dma((8, 2, pieces))] * 6,
+        dma((4, 2)), dma((4, 2)), dma((112,)), dma((112,)), dma((8,)),
     ]
     shape = jax.ShapeDtypeStruct
     shapes = (

time: 121 us -> 117 us (0.967)
  Pallas kernels: 120 us -> 116 us
    pallas_call x1, Pallas kernels: 118 us -> 114 us  [per_device(): pl.pallas_call(functools.partial(kernel, factor), out_shape=shapes, in_sp...]
where the time goes in v3:
time: 117 us
  Pallas kernels  116 us (99%)
    pallas_call x1, Pallas kernels, per_device(): pl.pallas_call(functools.partial(kernel, factor), out_shape=shapes, in_sp...  114 us

profile of v3, /device:TPU:2, one launch (start us, length us, event | category | flops | bytes accessed | tf_op | source)
XLA Modules:
  0.0 116.6 jit_solution(1077000785668806562)
XLA Ops:
  0.6 113.7 %block_backward.1 = (bf16[112,128]{1,0:T(8,128)(2,1)}, bf16[16,896]{1,0:T(8,128)(2,1)}, bf16[112,896]{1,0:T(8,128)(2,1)}, bf16[224,896]{1,0:T(8,128)(2,1)}, bf16[224,896]{1,0:T(8,128)(2,1)}) custom-call(bf16[112,128]{1,0:T(8,128)(2,1)} %bitcast.5, bf16[112,128]{1,0:T(8,128)(2,1)} %bitcast.6, bf16[16,896]{1,0:T(8,128)(2,1)} %attn_in.1, ...), custom_call_target="tpu_custom_call" | custom-call | flops 2500000000 | bytes 3000000 | tf_op jit(solution)/shard_map/block_backward/pallas_call | solution.py:487
  114.3 2.3 %write_out.1 = (bf16[112,128]{1,0:T(8,128)(2,1)}, bf16[16,896]{1,0:T(8,128)(2,1)}, bf16[112,896]{1,0:T(8,128)(2,1)}, bf16[224,896]{1,0:T(8,128)(2,1)}, bf16[224,896]{1,0:T(8,128)(2,1)}) custom-call(bf16[112,128]{1,0:T(8,128)(2,1)} %get-tuple-element.15.refs_0_, bf16[16,896]{1,0:T(8,128)(2,1)} %get-tuple-element.16.refs_1_, ...), custom_call_target="tpu_custom_call" | custom-call | bytes 3000000 | tf_op jit(solution)/shard_map/write_out/pallas_call | solution.py:502

commit v4 on v3

--- a/solution.py
+++ b/solution.py
@@ -153,15 +153,16 @@
     def block_from(d):
         return lax.rem(x - d + 4, 4)
 
-    h_copy = put(G.at[x, c, :, own_rows, :], G.at[x, c, :, own_rows, :], hpeer)
+    h_copy = [put(G.at[x, c, s, own_rows, :], G.at[x, c, s, own_rows, :], hpeer) for s in (1, 0)]
     own_y = [put(G.at[x, c, :, own_rows, :], G.at[x, c, :, own_rows, :], ypeer(d)) for d in near_first]
     gat_x = [[put(G.at[x, c, 1, own_rows, :], G.at[x, c, 1, own_rows, :], xpeer(d))] for d in near_first]
-    arrive(h_copy)
-    own_y += [
-        put(G.at[x, c, :, partner_rows, :], G.at[x, c, :, partner_rows, :], ypeer(d)) for d in near_first
-    ]
-    for copies, d in zip(gat_x, near_first):
-        copies.append(put(G.at[x, c, 1, partner_rows, :], G.at[x, c, 1, partner_rows, :], xpeer(d)))
+    for copy, s in zip(h_copy, (1, 0)):
+        arrive(copy)
+        arrived = G.at[x, c, s, partner_rows, :]
+        own_y += [put(arrived, arrived, ypeer(d)) for d in near_first]
+        if s:
+            for copies, d in zip(gat_x, near_first):
+                copies.append(put(arrived, arrived, xpeer(d)))
     own_attn = attn_all.at[attn_row, :]
     attn_z = [put(own_attn, own_attn, gxpeer(d)) for d in range(1, 8)]
     gate_copy = put(gates.at[h_rows, :], gates.at[h_rows, :], hpeer)

time: 117 us -> 116 us (level)
  the two profiles are of different devices: /device:TPU:2 before, /device:TPU:8 now
where the time goes in v4:
time: 116 us
  Pallas kernels  115 us (99%)
    pallas_call x1, Pallas kernels, per_device(): pl.pallas_call(functools.partial(kernel, factor), out_shape=shapes, in_sp...  113 us

profile of v4, /device:TPU:8, one launch (start us, length us, event | category | flops | bytes accessed | tf_op | source)
XLA Modules:
  0.0 115.6 jit_solution(13661622567364739229)
XLA Ops:
  0.6 112.7 %block_backward.1 = (bf16[112,128]{1,0:T(8,128)(2,1)}, bf16[16,896]{1,0:T(8,128)(2,1)}, bf16[112,896]{1,0:T(8,128)(2,1)}, bf16[224,896]{1,0:T(8,128)(2,1)}, bf16[224,896]{1,0:T(8,128)(2,1)}) custom-call(bf16[112,128]{1,0:T(8,128)(2,1)} %bitcast.5, bf16[112,128]{1,0:T(8,128)(2,1)} %bitcast.6, bf16[16,896]{1,0:T(8,128)(2,1)} %attn_in.1, ...), custom_call_target="tpu_custom_call" | custom-call | flops 2500000000 | bytes 3000000 | tf_op jit(solution)/shard_map/block_backward/pallas_call | solution.py:488
  113.4 2.3 %write_out.1 = (bf16[112,128]{1,0:T(8,128)(2,1)}, bf16[16,896]{1,0:T(8,128)(2,1)}, bf16[112,896]{1,0:T(8,128)(2,1)}, bf16[224,896]{1,0:T(8,128)(2,1)}, bf16[224,896]{1,0:T(8,128)(2,1)}) custom-call(bf16[112,128]{1,0:T(8,128)(2,1)} %get-tuple-element.15.refs_0_, bf16[16,896]{1,0:T(8,128)(2,1)} %get-tuple-element.16.refs_1_, ...), custom_call_target="tpu_custom_call" | custom-call | bytes 3000000 | tf_op jit(solution)/shard_map/write_out/pallas_call | solution.py:503

commit v5 on v4

--- a/solution.py
+++ b/solution.py
@@ -88,14 +88,12 @@
         copy.wait_recv()
         open_recv[:] = [other for other in open_recv if other is not copy]
 
-    def finish(line):
-        for copy in open_recv:
-            copy.wait_recv()
+    def settle_sent():
         for copy in sent:
             copy.wait_send()
-        if not line:
-            return
-
+        sent.clear()
+
+    def settle_line():
         for u in range(steps):
             for s in range(2):
                 for r in range(pieces):
@@ -142,20 +140,20 @@
         return jnp.broadcast_to(row[...].astype(F32), (toks, feats)).T
 
     G[x, c, 1, own_rows, :] = (og[...].astype(F32) * gate_columns(fg_row)).astype(BF16)
+
+    pl.semaphore_wait(barrier, len(peers))
+
+    near_first = (2, 1, 3)
+
+    def block_from(d):
+        return lax.rem(x - d + 4, 4)
+
+    h_copy = [put(G.at[x, c, s, own_rows, :], G.at[x, c, s, own_rows, :], hpeer) for s in (1, 0)]
+    own_y = [put(G.at[x, c, :, own_rows, :], G.at[x, c, :, own_rows, :], ypeer(d)) for d in near_first]
+    gat_x = [[put(G.at[x, c, 1, own_rows, :], G.at[x, c, 1, own_rows, :], xpeer(d))] for d in near_first]
     gates[h_rows, :] = gate_columns(ag_row).astype(BF16)
     for load in loads[4:]:
         load.wait()
-
-    pl.semaphore_wait(barrier, len(peers))
-
-    near_first = (2, 1, 3)
-
-    def block_from(d):
-        return lax.rem(x - d + 4, 4)
-
-    h_copy = [put(G.at[x, c, s, own_rows, :], G.at[x, c, s, own_rows, :], hpeer) for s in (1, 0)]
-    own_y = [put(G.at[x, c, :, own_rows, :], G.at[x, c, :, own_rows, :], ypeer(d)) for d in near_first]
-    gat_x = [[put(G.at[x, c, 1, own_rows, :], G.at[x, c, 1, own_rows, :], xpeer(d))] for d in near_first]
     for copy, s in zip(h_copy, (1, 0)):
         arrive(copy)
         arrived = G.at[x, c, s, partner_rows, :]
@@ -402,6 +400,8 @@
             arrive(copy)
             back[...] += proj_part(lax.rem(y - d + 4, 4) * 2 + n)
 
+    earlier = list(sent)
+    sent.clear()
     ap[...] = back[...].astype(BF16).reshape(ap.shape)
     ar_copies = [put(ap.at[lax.rem(a + d, 8)], ar.at[d - 1], gxpeer(d)) for d in (4, 3, 5, 2, 6, 1, 7)]
     gp_copies = []
@@ -409,6 +409,9 @@
         gp_copies.append(put(GM.at[feat_rows(lax.rem(gz + d, 8)), :], GP.at[gz], gzpeer(d)))
     GP[gz] = GM[feat_rows(gz), :]
     hand_over(attn_x, lambda block: attn_all.at[attn_rows(block), :], attn_c)
+    settle_line()
+    for copy in earlier:
+        copy.wait_send()
     for copy in attn_c:
         arrive(copy)
     for copy in gp_copies:
@@ -421,7 +424,7 @@
         total = total + ar[d].astype(F32)
     gattn_ref[...] = total.astype(BF16)
 
-    finish(True)
+    settle_sent()
 
 
 def write_out(*refs):

time: 116 us -> 116 us (level)
  no operation moved by 1% of the time
where the time goes in v5:
time: 116 us; the launch traced here: 115 us
  Pallas kernels  115 us (99%)
    pallas_call x1, Pallas kernels, per_device(): pl.pallas_call(functools.partial(kernel, factor), out_shape=shapes, in_sp...  113 us

profile of v5, /device:TPU:8, one launch (start us, length us, event | category | flops | bytes accessed | tf_op | source)
XLA Modules:
  0.0 115.4 jit_solution(1824501969443713696)
XLA Ops:
  0.6 112.5 %block_backward.1 = (bf16[112,128]{1,0:T(8,128)(2,1)}, bf16[16,896]{1,0:T(8,128)(2,1)}, bf16[112,896]{1,0:T(8,128)(2,1)}, bf16[224,896]{1,0:T(8,128)(2,1)}, bf16[224,896]{1,0:T(8,128)(2,1)}) custom-call(bf16[112,128]{1,0:T(8,128)(2,1)} %bitcast.5, bf16[112,128]{1,0:T(8,128)(2,1)} %bitcast.6, bf16[16,896]{1,0:T(8,128)(2,1)} %attn_in.1, ...), custom_call_target="tpu_custom_call" | custom-call | flops 2500000000 | bytes 3000000 | tf_op jit(solution)/shard_map/block_backward/pallas_call | solution.py:491
  113.2 2.3 %write_out.1 = (bf16[112,128]{1,0:T(8,128)(2,1)}, bf16[16,896]{1,0:T(8,128)(2,1)}, bf16[112,896]{1,0:T(8,128)(2,1)}, bf16[224,896]{1,0:T(8,128)(2,1)}, bf16[224,896]{1,0:T(8,128)(2,1)}) custom-call(bf16[112,128]{1,0:T(8,128)(2,1)} %get-tuple-element.15.refs_0_, bf16[16,896]{1,0:T(8,128)(2,1)} %get-tuple-element.16.refs_1_, ...), custom_call_target="tpu_custom_call" | custom-call | bytes 3000000 | tf_op jit(solution)/shard_map/write_out/pallas_call | solution.py:506
